TPU v7x, 32 devices: a whole 2x2x4 slice. The times are simulated.
32 devices in a mesh: row: 8 (over z, y), col: 4 (over x, core).
Axes of the slice: x: 2, y: 2, z: 4, core: 2. Of those that a mesh axis runs over, the one named last changes fastest.
Arguments:
- density: float32 [16, 4, 2, 128, 128], P('row', 'col'), as said below
- columns: int32 [16, 4, 2], P('row', 'col'), may hold values from -1 to 15, as said below
- owner_map: int32 [16], replicated, may hold values from 0 to 15, as said below
Outputs:
- purified: float32 [16, 4, 2, 128, 128], P('row', 'col')
Inputs may be any that keep to these rules, and one draw needn't show every extreme that they name: `columns`: entry [s, c, e] names by its global number a block column of block row s whose slot lies in c * 4 to (c + 1) * 4 - 1, or is -1 (empty). No block column is named twice in a row. The pattern is symmetric: if row s names a column with slot t, row t names the column with slot s. Each block row names its own diagonal block and the block whose slot differs from s in the lowest bit. A permutation: owner_map[g] is the slot (the position along the first dimension of the arrays) of the block with global number g. `density`: the matrix is symmetric: the block of row s at column slot t is the transpose of the block of row t at column slot s. Blocks at empty entries are not part of the matrix.
All inputs are finite; a program needn't handle non-finite values.
Results may differ from a plain program's by a relative error of at most 0.000054.
Values sent between devices are 32-bit elements; how exact they have to be, the bound alone decides.
A program may use at most 128 MiB of HBM per device.

v0:
```python
import jax
import jax.numpy as jnp
from jax import lax
from jax.sharding import PartitionSpec as P

HIGHEST_PRECISION = lax.Precision.HIGHEST


def slot_of(block_ids, owner_map):
    block_total = owner_map.shape[0]
    matches = block_ids[..., None] == jnp.arange(block_total, dtype=jnp.int32)
    slots = jnp.sum(jnp.where(matches, owner_map, 0), axis=-1)
    return (slots, block_ids >= 0)


def column_entries(stored, stored_slots, stored_valid, queries, asked, first_slot):
    index = jnp.where(asked, queries, 0)
    blocks = stored[index]
    local_col = stored_slots[index] - first_slot
    present = stored_valid[index] & asked[:, None]
    return (blocks, local_col, present)


def shards(density, columns, owner_map):
    rows_here = density.shape[0]
    entry_cap = density.shape[2]
    block_size = density.shape[3]
    group_total = lax.axis_size("col")
    block_total = owner_map.shape[0]
    group_width = block_total // group_total
    column_index = lax.axis_index("col")
    first_slot = column_index * group_width
    row_vals, row_ids = (
        lax.all_gather(density, "col", axis=1, tiled=True),
        lax.all_gather(columns, "col", axis=1, tiled=True),
    )
    row_slots, row_valid = slot_of(row_ids, owner_map)
    col_vals, col_ids = (
        lax.all_gather(density, "row", axis=0, tiled=True),
        lax.all_gather(columns, "row", axis=0, tiled=True),
    )
    stored = col_vals[:, 0]
    stored_slots, stored_valid = slot_of(col_ids[:, 0], owner_map)

    def entries(queries, asked):
        return column_entries(stored, stored_slots, stored_valid, queries, asked, first_slot)

    local_ids = jnp.arange(group_width, dtype=jnp.int32)
    blocks, local_col, present = entries(row_slots.reshape(-1), row_valid.reshape(-1))
    left_blocks = row_vals.reshape(-1, block_size, block_size)
    products = jnp.einsum("qab,qfbc->qfac", left_blocks, blocks, precision=HIGHEST_PRECISION)
    weight = ((local_col[..., None] == local_ids) & present[..., None]).astype(jnp.float32)
    weight = weight.reshape(rows_here, -1, entry_cap, group_width)
    products = products.reshape(rows_here, -1, entry_cap, block_size, block_size)
    square = jnp.einsum("iqft,iqfac->itac", weight, products, precision=HIGHEST_PRECISION)
    found, found_col, found_ok = entries(row_slots.reshape(-1), row_valid.reshape(-1))
    pick_weight = ((found_col[..., None] == local_ids) & found_ok[..., None]).astype(jnp.float32)
    pick_weight = pick_weight.reshape(
        rows_here, 1 * lax.axis_size("col") * entry_cap, entry_cap, group_width
    )
    picked = jnp.einsum("iqft,itac->iqfac", pick_weight, square, precision=HIGHEST_PRECISION)
    found = found.reshape(
        rows_here, 1 * lax.axis_size("col") * entry_cap, entry_cap, block_size, block_size
    )
    partial_value = jnp.einsum("iqfac,iqfbc->iqab", picked, found, precision=HIGHEST_PRECISION)
    partial_value = partial_value.reshape(
        rows_here, 1 * lax.axis_size("col"), entry_cap, block_size, block_size
    )
    cubic = lax.psum_scatter(
        jnp.transpose(partial_value, (1, 0, 2, 3, 4)), "col", scatter_dimension=0, tiled=True
    )[0]
    own_slots, own_valid = slot_of(columns[:, 0], owner_map)
    own_pick = (((own_slots - first_slot)[..., None] == local_ids) & own_valid[..., None]).astype(
        jnp.float32
    )
    square_own = jnp.einsum("ift,itac->ifac", own_pick, square, precision=HIGHEST_PRECISION)
    purified = (3.0 * square_own - 2.0 * cubic) * own_valid[..., None, None].astype(jnp.float32)
    return purified[:, None]


def solution(mesh):
    in_specs = (P("row", "col", None, None, None), P("row", "col", None), P())
    out_specs = P("row", "col", None, None, None)
    return jax.shard_map(shards, mesh=mesh, in_specs=in_specs, out_specs=out_specs, check_vma=False)
```

profile of v0, /device:TPU:0, one launch (start us, length us, event | category | flops | bytes accessed | tf_op | source)
XLA Modules:
  0.0 128.8 jit_solution(2024190081916549478)
XLA Ops:
  6.5 0.7 all-gather.3.cloned.1.call-update
  7.3 0.7 all-gather.5.cloned.1.call-update
  8.1 6.3 %all_gather.13 = s32[2,4,2]{2,0,1:T(2,128)S(1)} all-gather(s32[2,1,2]{2,0,1:T(2,128)} %bitcast.64), channel_id=1, replica_groups=mesh['row'=8,'col'=4] {'col'}, dimensions={1}, use_global_device_ids=true | all-gather | bytes 80 | tf_op jit(solution)/shard_map/all_gather | solution.py:35
  14.4 0.9 select_reduce_fusion.1
  15.5 21.6 %all_gather.12 = s32[16,1,2]{2,1,0:T(1,128)S(1)} all-gather(s32[2,1,2]{2,1,0:T(1,128)} %param.4), channel_id=1, replica_groups=mesh['row'=8,'col'=4] {'row'}, dimensions={0}, use_global_device_ids=true | all-gather | bytes 144 | tf_op jit(solution)/shard_map/all_gather | solution.py:40
  37.2 0.6 gather_fusion.1
  37.8 0.1 copy.86
  37.9 0.1 copy.70
  38.1 0.8 select_reduce_fusion
  39.1 0.6 gather_fusion
  39.7 21.8 %all-gather.3.cloned.1.call-done = f32[16,1,2,128,128]{4,3,2,1,0:T(8,128)} async-done(((f32[2,1,2,128,128]{4,3,2,1,0:T(8,128)}), f32[16,1,2,128,128]{4,3,2,1,0:T(8,128)}) %all-gather.3.cloned.1.call-update) | async-done | bytes 2097168 | tf_op jit(solution)/shard_map/all_gather | solution.py:39
  61.6 2.3 %gather_fusion.2 = f32[16,2,128,128]{3,2,1,0:T(8,128)S(1)} fusion(f32[16,2,128,128]{3,2,1,0:T(8,128)} %bitcast.62, s32[1024]{0:T(1024)S(1)} %pad_clamp_fusion), kind=kCustom, calls=%fused_computation.2 | custom fusion | bytes 4194368 | tf_op jit(solution)/shard_map/gather | solution.py:18
  63.8 14.5 %all-gather.5.cloned.1.call-done = f32[2,4,2,128,128]{4,3,2,1,0:T(8,128)} async-done(((f32[2,1,2,128,128]{4,3,2,1,0:T(8,128)}), f32[2,4,2,128,128]{4,3,2,1,0:T(8,128)}) %all-gather.5.cloned.1.call-update) | async-done | bytes 1048592 | tf_op jit(solution)/shard_map/all_gather | solution.py:34
  78.4 6.3 %fusion.28 = f32[16,2,128,128]{3,2,1,0:T(8,128)} fusion(f32[16,2,128,128]{3,2,1,0:T(8,128)S(1)} %gather_fusion.2, f32[16,128,128,1]{2,1,3,0:T(8,128)} %bitcast.63), kind=kOutput, calls=%fused_computation.47 | convolution fusion | flops 805306368 | bytes 5242880 | tf_op jit(solution)/shard_map/qab,qfbc->qfac/dot_general | solution.py:51
  84.7 3.0 %copy.73 = f32[2,8,2,128,128]{4,1,2,3,0:T(8,128)} copy(f32[2,8,2,128,128]{3,4,2,1,0:T(8,128)} %bitcast.60) | data formatting | bytes 4194304 | tf_op jit(solution)/shard_map/reshape | solution.py:54
  87.7 2.5 %fusion.10 = f32[2,4,128,128,1]{3,1,4,2,0:T(4,128)S(1)} fusion(f32[2,8,2,128,128]{4,1,2,3,0:T(8,128)} %copy.73, s32[2,8,2]{1,2,0:T(2,128)S(1)} %copy.67, pred[2,8,2]{1,2,0:T(4,128)(4,1)S(1)} %copy.71), kind=kOutput, calls=%fused_computation.21 | convolution fusion | flops 25166080 | bytes 2621600 | tf_op jit(solution)/shard_map/iqft,iqfac->itac/dot_general | solution.py:55
  90.3 1.1 fusion.5
  91.3 2.2 %fusion = f32[2,8,128,128,1]{3,2,4,1,0:T(8,128)S(1)} fusion(f32[2,8,2,128,128]{4,3,2,1,0:T(8,128)S(1)} %bitcast.59, f32[2,8,2,128,128]{4,1,3,2,0:T(8,128)S(1)} %fusion.5), kind=kOutput, calls=%fused_computation.3 | convolution fusion | flops 805306368 | bytes 5242880 | tf_op jit(solution)/shard_map/iqfac,iqfbc->iqab/dot_general | solution.py:65
  93.6 1.0 copy.75
  94.7 0.2 fusion.21
  94.9 24.8 %reduce-scatter.2.cloned.1.call-done = f32[1,2,2,128,128]{4,3,2,1,0:T(8,128)} async-done(((f32[4,2,2,128,128]{4,3,2,1,0:T(8,128)}), f32[1,2,2,128,128]{4,3,2,1,0:T(8,128)}) %reduce-scatter.2.cloned.1.call-update) | async-done | bytes 262160 | tf_op jit(solution)/shard_map/reduce_scatter | solution.py:69
  119.7 1.0 broadcast_multiply_fusion
  120.7 0.8 fusion.4
  121.5 0.7 copy.77
  (25 shorter events, 0.9 us)
Async XLA Ops:
  6.5 55.0 %all-gather.3.cloned.1.call-start = ((), (), s32[]{:S(2)}) async-start(), calls=%async_computation.1 | async-start | bytes 2359296 | tf_op jit(solution)/shard_map/all_gather | solution.py:39
  7.3 71.1 %all-gather.5.cloned.1.call-start = ((), (), s32[]{:S(2)}) async-start(), calls=%async_computation.2 | async-start | bytes 1310720 | tf_op jit(solution)/shard_map/all_gather | solution.py:34
  8.0 111.7 %reduce-scatter.2.cloned.1.call-start = ((), (), s32[]{:S(2)}) async-start(), calls=%async_computation.3 | async-start | bytes 1310720 | tf_op jit(solution)/shard_map/reduce_scatter | solution.py:69
  93.6 1.1 copy-start
  93.6 1.1 copy-start.1
Sparse Core Ops, SparseCore 0:
  9.5 52.0 all-gather.2
  63.1 15.1 all-gather.4
  94.8 24.8 reduce-scatter.1
where the time goes:
time: 129 us
  waiting for transfers between devices  62.5 us (48%)
  blocking collectives  27.8 us (22%)
  between operations  13.2 us (10%)
  matrix products  13 us (10%)
  local copies, waits for them, and re-layouts  9.19 us (7%)
  other arithmetic  2.95 us (2%)
    reduce_scatter x1, waiting for transfers between devices, shards(): lax.psum_scatter(jnp.transpose(partial_value, (1, 0, 2, 3, 4)), 'col', sc...  24.8 us
    all_gather x1, waiting for transfers between devices, shards(): lax.all_gather(density, 'row', axis=0, tiled=True)  21.8 us
    all_gather x1, blocking collectives, shards(): lax.all_gather(columns, 'row', axis=0, tiled=True)  21.6 us
    all_gather x1, waiting for transfers between devices, shards(): lax.all_gather(density, 'col', axis=1, tiled=True)  14.5 us
    dot_general x1, matrix products, shards(): jnp.einsum('qab,qfbc->qfac', left_blocks, blocks, precision=HIGHEST_PRECI...  6.33 us
    all_gather x1, blocking collectives, shards(): lax.all_gather(columns, 'col', axis=1, tiled=True)  6.25 us
    reshape x1, local copies, waits for them, and re-layouts, shards(): products.reshape(rows_here, -1, entry_cap, block_size, block_size)  3.04 us
  transfers between devices with their start and end apart: 3, of which 3 were waited for; matrix products, arithmetic and copies ran while one was open for 5% of the time, Pallas kernels for 0%

commit v1 on v0

--- a/solution.py
+++ b/solution.py
@@ -1,9 +1,13 @@
 import jax
 import jax.numpy as jnp
 from jax import lax
+from jax.experimental import pallas as pl
+from jax.experimental.pallas import tpu as pltpu
 from jax.sharding import PartitionSpec as P
 
 HIGHEST_PRECISION = lax.Precision.HIGHEST
+MESH = pl.DeviceIdType.MESH
+GROUPS = 4
 
 
 def slot_of(block_ids, owner_map):
@@ -78,7 +82,283 @@
     return purified[:, None]
 
 
+def chosen(group, col):
+    step = (col - group + GROUPS) % GROUPS
+    middle = jnp.logical_or(group == 1, group == 2)
+    return jnp.logical_or(step <= 1, jnp.logical_and(step == 2, middle))
+
+
+def split(value):
+    high = value.astype(jnp.bfloat16)
+    low = (value - high.astype(jnp.float32)).astype(jnp.bfloat16)
+    return high, low
+
+
+def gather_kernel(
+    den_ref, cols_ref, owner_ref, out_ref, units, mat_h, mat_l, sq_h, sq_l, sq_own, send_sem, recv_sem
+):
+    size = den_ref.shape[-1]
+    row = lax.axis_index("row")
+    col = lax.axis_index("col")
+    z, y = row // 2, row % 2
+    x, core = col // 2, col % 2
+
+    def device(z_at, y_at, x_at, core_at):
+        return {"row": z_at * 2 + y_at, "col": x_at * 2 + core_at}
+
+    targets = {
+        0: device(z + 1, y, x, core),
+        1: device(z - 1, y, x, core),
+        2: device(z, y, 1 - x, core),
+        3: device(z, 1 - y, x, core),
+        4: device(z, y, x, 1 - core),
+    }
+    there = {0: z < GROUPS - 1, 1: z > 0}
+
+    barrier = pltpu.get_barrier_semaphore()
+    for kind, target in targets.items():
+        if kind in there:
+
+            @pl.when(there[kind])
+            def _():
+                pl.semaphore_signal(barrier, inc=1, device_id=target, device_id_type=MESH)
+        else:
+            pl.semaphore_signal(barrier, inc=1, device_id=target, device_id_type=MESH)
+
+    slots = []
+    for i in range(2):
+        pair = []
+        for e in range(2):
+            name = cols_ref[i, 0, e]
+            place = owner_ref[jnp.maximum(name, 0)] - col * GROUPS
+            pair.append(jnp.where(name >= 0, place, -1))
+        slots.append(pair)
+        own = units.at[row * 2 + i, col]
+        for e in range(2):
+            own[e * size : (e + 1) * size, :] = den_ref[i, 0, e]
+        sub = lax.broadcasted_iota(jnp.int32, (8, size), 0)
+        own[2 * size : 2 * size + 8, :] = jnp.where(sub == 0, pair[0], pair[1]).astype(jnp.float32)
+
+    pl.semaphore_wait(barrier, 3 + there[0].astype(jnp.int32) + there[1].astype(jnp.int32))
+
+    sends = []
+
+    def copy(kind, s, c):
+        return pltpu.make_async_remote_copy(
+            src_ref=units.at[s, c],
+            dst_ref=units.at[s, c],
+            send_sem=send_sem.at[kind, s, c],
+            recv_sem=recv_sem.at[s, c],
+            device_id=targets[kind],
+            device_id_type=MESH,
+        )
+
+    def start(kind, s, c, guard):
+        pred = guard
+        if kind in there:
+            pred = jnp.logical_and(guard, there[kind])
+
+        @pl.when(pred)
+        def _():
+            copy(kind, s, c).start()
+
+        sends.append((pred, kind, s, c))
+
+    def arrive(s, c, guard):
+        @pl.when(guard)
+        def _():
+            copy(2, s, c).wait_recv()
+
+    def planes(distance):
+        if distance == 0:
+            return [(z, jnp.bool_(True), None)]
+        return [
+            (z - distance, z - distance >= 0, 0),
+            (z + distance, z + distance < GROUPS, 1),
+        ]
+
+    def lane(distance):
+        for plane, inside, way in planes(distance):
+            guard = jnp.logical_and(inside, chosen(plane, col))
+            for h in range(2):
+                s = plane * 4 + y * 2 + h
+                if distance:
+                    arrive(s, col, guard)
+                for kind in (0, 1) if way is None else (way,):
+                    start(kind, s, col, guard)
+                for kind in (2, 3) if h == 0 else (3, 2):
+                    start(kind, s, col, guard)
+                start(4, s, col, guard)
+
+    def near(distance):
+        for plane, inside, _ in planes(distance):
+            other = (1 - x) * 2 + core
+            guard_x = jnp.logical_and(inside, chosen(plane, other))
+            guard_y = jnp.logical_and(inside, chosen(plane, col))
+            s = plane * 4 + y * 2
+            t = plane * 4 + (1 - y) * 2
+            arrive(s, other, guard_x)
+            start(3, s, other, guard_x)
+            start(4, s, other, guard_x)
+            arrive(t + 1, col, guard_y)
+            start(2, t + 1, col, guard_y)
+            start(4, t + 1, col, guard_y)
+            arrive(s + 1, other, guard_x)
+            start(4, s + 1, other, guard_x)
+            arrive(t, col, guard_y)
+            start(4, t, col, guard_y)
+
+    def corner(distance):
+        for plane, inside, _ in planes(distance):
+            other = (1 - x) * 2 + core
+            guard = jnp.logical_and(inside, chosen(plane, other))
+            for h in range(2):
+                s = plane * 4 + (1 - y) * 2 + h
+                arrive(s, other, guard)
+                start(4, s, other, guard)
+
+    def twin(distance):
+        for plane, inside, _ in planes(distance):
+            for x_at in range(2):
+                other = x_at * 2 + 1 - core
+                guard = jnp.logical_and(inside, chosen(plane, other))
+                for i in range(4):
+                    arrive(plane * 4 + i, other, guard)
+
+    def dense(distance):
+        for plane, inside, _ in planes(distance):
+            for step in range(3):
+                c = (plane + step) % GROUPS
+                guard = inside
+                if step == 2:
+                    guard = jnp.logical_and(inside, chosen(plane, c))
+
+                @pl.when(guard)
+                def _():
+                    @pl.loop(0, 4)
+                    def _(i):
+                        s = plane * 4 + i
+                        unit = units.at[s, c]
+                        places = [unit[2 * size + e : 2 * size + e + 1, :] for e in range(2)]
+                        at_s = pl.ds(pl.multiple_of(s * size, size), size)
+                        for way in range(1 if step == 0 else 2):
+                            blocks = [unit[e * size : (e + 1) * size, :] for e in range(2)]
+                            if way:
+                                blocks = [b.T for b in blocks]
+                            for j in range(4):
+                                at_j = pl.ds(pl.multiple_of((c * 4 + j) * size, size), size)
+                                value = jnp.where(
+                                    places[0] == j,
+                                    blocks[0],
+                                    jnp.where(places[1] == j, blocks[1], 0.0),
+                                )
+                                high, low = split(value)
+                                if way:
+                                    mat_h[at_j, at_s] = high
+                                    mat_l[at_j, at_s] = low
+                                else:
+                                    mat_h[at_s, at_j] = high
+                                    mat_l[at_s, at_j] = low
+
+    lane(0)
+    lane(1)
+    near(0)
+    lane(2)
+    near(1)
+    corner(0)
+    lane(3)
+    near(2)
+    corner(1)
+    twin(0)
+    dense(0)
+    near(3)
+    corner(2)
+    twin(1)
+    dense(1)
+    corner(3)
+    twin(2)
+    dense(2)
+    twin(3)
+    dense(3)
+
+    width = GROUPS * size
+
+    def dot(a, b):
+        return jnp.dot(a, b, preferred_element_type=jnp.float32)
+
+    rows = pl.ds(pl.multiple_of(row * 2 * size, 2 * size), 2 * size)
+
+    @pl.loop(0, GROUPS)
+    def _(n):
+        at = pl.ds(pl.multiple_of(n * width, width), width)
+        a_h, a_l = mat_h[rows, :], mat_l[rows, :]
+        part = dot(a_h, mat_h[:, at])
+        part += dot(a_l, mat_h[:, at])
+        part += dot(a_h, mat_l[:, at])
+        high, low = split(part)
+        sq_h[:, at] = high
+        sq_l[:, at] = low
+
+    at = pl.ds(pl.multiple_of(col * width, width), width)
+    cube = dot(sq_h[...], mat_h[:, at])
+    cube += dot(sq_l[...], mat_h[:, at])
+    cube += dot(sq_h[...], mat_l[:, at])
+    square = sq_h[:, at].astype(jnp.float32) + sq_l[:, at].astype(jnp.float32)
+    sq_own[...] = 3.0 * square - 2.0 * cube
+    for i in range(2):
+        for e in range(2):
+            value = jnp.zeros((size, size), jnp.float32)
+            for j in range(4):
+                block = sq_own[i * size : (i + 1) * size, j * size : (j + 1) * size]
+                value = jnp.where(jnp.full((1, size), slots[i][e], jnp.int32) == j, block, value)
+            out_ref[i, 0, e] = value
+
+    for pred, kind, s, c in sends:
+
+        @pl.when(pred)
+        def _():
+            copy(kind, s, c).wait_send()
+
+
+def gathered(density, columns, owner_map):
+    size = density.shape[3]
+    total = owner_map.shape[0]
+    width = GROUPS * size
+    full = total * size
+    return pl.pallas_call(
+        gather_kernel,
+        out_shape=jax.ShapeDtypeStruct(density.shape, jnp.float32),
+        in_specs=[
+            pl.BlockSpec(memory_space=pltpu.VMEM),
+            pl.BlockSpec(memory_space=pltpu.SMEM),
+            pl.BlockSpec(memory_space=pltpu.SMEM),
+        ],
+        out_specs=pl.BlockSpec(memory_space=pltpu.VMEM),
+        scratch_shapes=[
+            pltpu.VMEM((total, GROUPS, 2 * size + 8, size), jnp.float32),
+            pltpu.VMEM((full, full), jnp.bfloat16),
+            pltpu.VMEM((full, full), jnp.bfloat16),
+            pltpu.VMEM((2 * size, full), jnp.bfloat16),
+            pltpu.VMEM((2 * size, full), jnp.bfloat16),
+            pltpu.VMEM((2 * size, width), jnp.float32),
+            pltpu.SemaphoreType.DMA((5, total, GROUPS)),
+            pltpu.SemaphoreType.DMA((total, GROUPS)),
+        ],
+        compiler_params=pltpu.CompilerParams(
+            collective_id=0, has_side_effects=True, vmem_limit_bytes=48 * 2**20
+        ),
+    )(density, columns, owner_map)
+
+
 def solution(mesh):
     in_specs = (P("row", "col", None, None, None), P("row", "col", None), P())
     out_specs = P("row", "col", None, None, None)
-    return jax.shard_map(shards, mesh=mesh, in_specs=in_specs, out_specs=out_specs, check_vma=False)
+    small = mesh.shape["row"] == 2 * GROUPS and mesh.shape["col"] == GROUPS
+
+    def program(density, columns, owner_map):
+        fits = small and owner_map.shape[0] == 4 * GROUPS and density.shape[:3] == (2, 1, 2)
+        if fits and density.shape[3] % 128 == 0 and density.shape[3] <= 128:
+            return gathered(density, columns, owner_map)
+        return shards(density, columns, owner_map)
+
+    return jax.shard_map(program, mesh=mesh, in_specs=in_specs, out_specs=out_specs, check_vma=False)

time: 129 us -> 54.8 us (0.42)
  waiting for transfers between devices: 62.5 us -> 0 us
  Pallas kernels: 0 us -> 50.8 us
  blocking collectives: 27.8 us -> 0 us
  between operations: 13.2 us -> 0.01 us
  matrix products: 13 us -> 0 us
  local copies, waits for them, and re-layouts: 9.19 us -> 2.99 us
  other arithmetic: 2.95 us -> 0 us
    pallas_call x0 -> x1, Pallas kernels: none -> 50.8 us  [gathered(): pl.pallas_call(gather_kernel, out_shape=jax.ShapeDtypeStruct(density.shap...]
    all_gather x2 -> x0, waiting for transfers between devices: 36.3 us -> none  [the longest x1 21.8 us: shards(): lax.all_gather(density, 'row', axis=0, tiled=True)]
    all_gather x2 -> x0, blocking collectives: 27.8 us -> none  [the longest x1 21.6 us: shards(): lax.all_gather(columns, 'row', axis=0, tiled=True)]
    reduce_scatter x1 -> x0, waiting for transfers between devices: 24.8 us -> none  [shards(): lax.psum_scatter(jnp.transpose(partial_value, (1, 0, 2, 3, 4)), 'col', sc...]
    dot_general x5 -> x0, matrix products: 13 us -> none  [the longest x1 6.33 us: shards(): jnp.einsum('qab,qfbc->qfac', left_blocks, blocks, precision=HIGHEST_PRECI...]
    gather x4 -> x0, local copies, waits for them, and re-layouts: 3.52 us -> none  [the longest x1 2.27 us: column_entries(): blocks = stored[index]]
    reshape x1 -> x0, local copies, waits for them, and re-layouts: 3.04 us -> none  [shards(): products.reshape(rows_here, -1, entry_cap, block_size, block_size)]
    unnamed x4 -> x7, local copies, waits for them, and re-layouts: 0.01 us -> 2.99 us
  transfers between devices with their start and end apart: 3 -> 0, of which waited for: 3 -> 0; matrix products, arithmetic and copies ran while one was open for 5% -> 0% of each run, Pallas kernels for 0% -> 0%
where the time goes in v1:
time: 54.8 us; the launch traced here: 53.8 us
  Pallas kernels  50.8 us (93%)
  local copies, waits for them, and re-layouts  2.99 us (5%)
    pallas_call x1, Pallas kernels, gathered(): pl.pallas_call(gather_kernel, out_shape=jax.ShapeDtypeStruct(density.shap...  50.8 us
    unnamed x7, local copies, waits for them, and re-layouts  2.99 us

profile of v1, /device:TPU:0, one launch (start us, length us, event | category | flops | bytes accessed | tf_op | source)
XLA Modules:
  0.0 53.8 jit_solution(2438001688173289316)
XLA Ops:
  0.0 0.0 copy-start
  0.0 0.9 %copy-done = f32[2,1,2,128,128]{4,3,2,1,0:T(8,128)S(1)} copy-done((f32[2,1,2,128,128]{4,3,2,1,0:T(8,128)S(1)}, f32[2,1,2,128,128]{4,3,2,1,0:T(8,128)}, u32[]{:S(2)}) %copy-start) | copy-done | bytes 262168
  1.0 0.0 copy-start.1
  1.0 0.7 %copy-done.1 = s32[2,1,2]{2,1,0:T(1,128)S(1)} copy-done((s32[2,1,2]{2,1,0:T(1,128)S(1)}, s32[2,1,2]{2,1,0:T(1,128)}, u32[]{:S(2)}) %copy-start.1) | copy-done | bytes 40
  1.6 0.0 copy-start.2
  1.6 0.7 %copy-done.2 = s32[16]{0:T(128)S(1)} copy-done((s32[16]{0:T(128)S(1)}, s32[16]{0:T(128)}, u32[]{:S(2)}) %copy-start.2) | copy-done | bytes 88
  2.3 50.8 %shard_map.37 = f32[2,1,2,128,128]{4,3,2,1,0:T(8,128)S(1)} custom-call(f32[2,1,2,128,128]{4,3,2,1,0:T(8,128)S(1)} %copy-done, s32[2,1,2]{2,1,0:T(1,128)S(1)} %copy-done.1, s32[16]{0:T(128)S(1)} %copy-done.2), custom_call_target="tpu_custom_call" | custom-call | tf_op jit(solution)/shard_map/pallas_call | solution.py:328
  53.1 0.7 %copy.5 = f32[2,1,2,128,128]{4,3,2,1,0:T(8,128)} copy(f32[2,1,2,128,128]{4,3,2,1,0:T(8,128)S(1)} %shard_map.37) | data formatting | bytes 524288
Async XLA Ops:
  0.0 0.9 %copy-start = (f32[2,1,2,128,128]{4,3,2,1,0:T(8,128)S(1)}, f32[2,1,2,128,128]{4,3,2,1,0:T(8,128)}, u32[]{:S(2)}) copy-start(f32[2,1,2,128,128]{4,3,2,1,0:T(8,128)} %den_ref.1) | copy-start | bytes 786436
  1.0 0.7 %copy-start.1 = (s32[2,1,2]{2,1,0:T(1,128)S(1)}, s32[2,1,2]{2,1,0:T(1,128)}, u32[]{:S(2)}) copy-start(s32[2,1,2]{2,1,0:T(1,128)} %cols_ref.1) | copy-start | bytes 52
  1.6 0.7 %copy-start.2 = (s32[16]{0:T(128)S(1)}, s32[16]{0:T(128)}, u32[]{:S(2)}) copy-start(s32[16]{0:T(128)} %owner_ref.1) | copy-start | bytes 196

commit v2 on v1

--- a/solution.py
+++ b/solution.py
@@ -1,3 +1,5 @@
+import functools
+
 import jax
 import jax.numpy as jnp
 from jax import lax
@@ -82,10 +84,12 @@
     return purified[:, None]
 
 
+CHOSEN = (0, 2, 4, 5, 7, 9, 10, 11, 12, 15)
+
+
 def chosen(group, col):
-    step = (col - group + GROUPS) % GROUPS
-    middle = jnp.logical_or(group == 1, group == 2)
-    return jnp.logical_or(step <= 1, jnp.logical_and(step == 2, middle))
+    place = group * GROUPS + col
+    return functools.reduce(jnp.logical_or, [place == n for n in CHOSEN])
 
 
 def split(value):
@@ -95,7 +99,23 @@
 
 
 def gather_kernel(
-    den_ref, cols_ref, owner_ref, out_ref, units, mat_h, mat_l, sq_h, sq_l, sq_own, send_sem, recv_sem
+    den_ref,
+    cols_ref,
+    owner_ref,
+    out_ref,
+    units,
+    mat_h,
+    mat_l,
+    square,
+    sq_h,
+    sq_l,
+    sq_own,
+    given,
+    taken,
+    send_sem,
+    recv_sem,
+    local_sem,
+    trade_sem,
 ):
     size = den_ref.shape[-1]
     row = lax.axis_index("row")
@@ -125,7 +145,19 @@
         else:
             pl.semaphore_signal(barrier, inc=1, device_id=target, device_id_type=MESH)
 
+    large = [
+        pltpu.make_async_copy(
+            den_ref.at[i, 0, e],
+            units.at[row * 2 + i, col, pl.ds(e * size, size)],
+            local_sem.at[i * 2 + e],
+        )
+        for i in range(2)
+        for e in range(2)
+    ]
+    for item in large:
+        item.start()
     slots = []
+    sub = lax.broadcasted_iota(jnp.int32, (8, size), 0)
     for i in range(2):
         pair = []
         for e in range(2):
@@ -134,10 +166,9 @@
             pair.append(jnp.where(name >= 0, place, -1))
         slots.append(pair)
         own = units.at[row * 2 + i, col]
-        for e in range(2):
-            own[e * size : (e + 1) * size, :] = den_ref[i, 0, e]
-        sub = lax.broadcasted_iota(jnp.int32, (8, size), 0)
         own[2 * size : 2 * size + 8, :] = jnp.where(sub == 0, pair[0], pair[1]).astype(jnp.float32)
+    for item in large:
+        item.wait()
 
     pl.semaphore_wait(barrier, 3 + there[0].astype(jnp.int32) + there[1].astype(jnp.int32))
 
@@ -180,15 +211,18 @@
     def lane(distance):
         for plane, inside, way in planes(distance):
             guard = jnp.logical_and(inside, chosen(plane, col))
+            s = plane * 4 + y * 2
+            ways = (0, 1) if way is None else (way,)
             for h in range(2):
-                s = plane * 4 + y * 2 + h
                 if distance:
-                    arrive(s, col, guard)
-                for kind in (0, 1) if way is None else (way,):
-                    start(kind, s, col, guard)
-                for kind in (2, 3) if h == 0 else (3, 2):
-                    start(kind, s, col, guard)
-                start(4, s, col, guard)
+                    arrive(s + h, col, guard)
+                for kind in ways:
+                    start(kind, s + h, col, guard)
+                start(2 + h, s + h, col, guard)
+            start(3, s, col, guard)
+            start(2, s + 1, col, guard)
+            for h in range(2):
+                start(4, s + h, col, guard)
 
     def near(distance):
         for plane, inside, _ in planes(distance):
@@ -227,11 +261,9 @@
 
     def dense(distance):
         for plane, inside, _ in planes(distance):
-            for step in range(3):
+            for step in range(4):
                 c = (plane + step) % GROUPS
-                guard = inside
-                if step == 2:
-                    guard = jnp.logical_and(inside, chosen(plane, c))
+                guard = jnp.logical_and(inside, chosen(plane, c))
 
                 @pl.when(guard)
                 def _():
@@ -260,51 +292,102 @@
                                     mat_h[at_s, at_j] = high
                                     mat_l[at_s, at_j] = low
 
+    width = GROUPS * size
+
+    def dot(a, b):
+        return jnp.dot(a, b, preferred_element_type=jnp.float32)
+
+    rows = pl.ds(pl.multiple_of(row * 2 * size, 2 * size), 2 * size)
+
+    def group_at(group):
+        return pl.ds(pl.multiple_of(group * width, width), width)
+
+    def away(a, b):
+        gap = jnp.where(chosen(a, b), a, b) - z
+        return jnp.maximum(gap, -gap)
+
+    def squared(distance):
+        @pl.loop(0, GROUPS * 2)
+        def _(n):
+            a, b = n // 2, (n % 2) * 2 + core
+
+            @pl.when(jnp.maximum(away(z, a), away(a, b)) == distance)
+            def _():
+                at_a, at_b = group_at(a), group_at(b)
+                a_h, a_l = mat_h[rows, at_a], mat_l[rows, at_a]
+                part = dot(a_h, mat_h[at_a, at_b])
+                part += dot(a_l, mat_h[at_a, at_b])
+                part += dot(a_h, mat_l[at_a, at_b])
+                square[:, at_b] += part
+
+    def flush(keep):
+        while len(sends) > keep:
+            pred, kind, s, c = sends.pop(0)
+
+            @pl.when(pred)
+            def _():
+                copy(kind, s, c).wait_send()
+
+    def compute(distance):
+        twin(distance)
+        dense(distance)
+        squared(distance)
+
     lane(0)
+    square[...] = jnp.zeros_like(square)
     lane(1)
     near(0)
     lane(2)
     near(1)
     corner(0)
+    twin(0)
+    dense(0)
     lane(3)
     near(2)
     corner(1)
-    twin(0)
-    dense(0)
+    squared(0)
+    twin(1)
+    dense(1)
     near(3)
     corner(2)
-    twin(1)
-    dense(1)
-    corner(3)
+    squared(1)
     twin(2)
     dense(2)
-    twin(3)
-    dense(3)
-
-    width = GROUPS * size
-
-    def dot(a, b):
-        return jnp.dot(a, b, preferred_element_type=jnp.float32)
-
-    rows = pl.ds(pl.multiple_of(row * 2 * size, 2 * size), 2 * size)
-
-    @pl.loop(0, GROUPS)
-    def _(n):
-        at = pl.ds(pl.multiple_of(n * width, width), width)
-        a_h, a_l = mat_h[rows, :], mat_l[rows, :]
-        part = dot(a_h, mat_h[:, at])
-        part += dot(a_l, mat_h[:, at])
-        part += dot(a_h, mat_l[:, at])
-        high, low = split(part)
-        sq_h[:, at] = high
-        sq_l[:, at] = low
-
-    at = pl.ds(pl.multiple_of(col * width, width), width)
-    cube = dot(sq_h[...], mat_h[:, at])
-    cube += dot(sq_l[...], mat_h[:, at])
-    cube += dot(sq_h[...], mat_l[:, at])
-    square = sq_h[:, at].astype(jnp.float32) + sq_l[:, at].astype(jnp.float32)
-    sq_own[...] = 3.0 * square - 2.0 * cube
+    flush(60)
+    corner(3)
+    squared(2)
+    flush(20)
+    compute(3)
+
+    @pl.loop(0, 2)
+    def _(half):
+        at = group_at(half * 2 + core)
+        sq_h[:, at], sq_l[:, at] = split(square[:, at])
+
+    def share(group):
+        total = None
+        for half in range(2):
+            at_q, at = group_at(half * 2 + core), group_at(group)
+            part = dot(sq_h[:, at_q], mat_h[at_q, at])
+            part += dot(sq_l[:, at_q], mat_h[at_q, at])
+            part += dot(sq_h[:, at_q], mat_l[at_q, at])
+            total = part if total is None else total + part
+        return total
+
+    trade = pltpu.make_async_remote_copy(
+        src_ref=given,
+        dst_ref=taken,
+        send_sem=trade_sem.at[0],
+        recv_sem=trade_sem.at[1],
+        device_id=targets[4],
+        device_id_type=MESH,
+    )
+    given[...] = share(x * 2 + 1 - core)
+    trade.start()
+    sq_own[...] = 3.0 * square[:, group_at(col)] - 2.0 * share(col)
+    flush(0)
+    trade.wait()
+    sq_own[...] -= 2.0 * taken[...]
     for i in range(2):
         for e in range(2):
             value = jnp.zeros((size, size), jnp.float32)
@@ -312,12 +395,6 @@
                 block = sq_own[i * size : (i + 1) * size, j * size : (j + 1) * size]
                 value = jnp.where(jnp.full((1, size), slots[i][e], jnp.int32) == j, block, value)
             out_ref[i, 0, e] = value
-
-    for pred, kind, s, c in sends:
-
-        @pl.when(pred)
-        def _():
-            copy(kind, s, c).wait_send()
 
 
 def gathered(density, columns, owner_map):
@@ -329,7 +406,7 @@
         gather_kernel,
         out_shape=jax.ShapeDtypeStruct(density.shape, jnp.float32),
         in_specs=[
-            pl.BlockSpec(memory_space=pltpu.VMEM),
+            pl.BlockSpec(memory_space=pltpu.HBM),
             pl.BlockSpec(memory_space=pltpu.SMEM),
             pl.BlockSpec(memory_space=pltpu.SMEM),
         ],
@@ -338,14 +415,19 @@
             pltpu.VMEM((total, GROUPS, 2 * size + 8, size), jnp.float32),
             pltpu.VMEM((full, full), jnp.bfloat16),
             pltpu.VMEM((full, full), jnp.bfloat16),
+            pltpu.VMEM((2 * size, full), jnp.float32),
             pltpu.VMEM((2 * size, full), jnp.bfloat16),
             pltpu.VMEM((2 * size, full), jnp.bfloat16),
             pltpu.VMEM((2 * size, width), jnp.float32),
+            pltpu.VMEM((2 * size, width), jnp.float32),
+            pltpu.VMEM((2 * size, width), jnp.float32),
             pltpu.SemaphoreType.DMA((5, total, GROUPS)),
             pltpu.SemaphoreType.DMA((total, GROUPS)),
+            pltpu.SemaphoreType.DMA((4,)),
+            pltpu.SemaphoreType.DMA((2,)),
         ],
         compiler_params=pltpu.CompilerParams(
-            collective_id=0, has_side_effects=True, vmem_limit_bytes=48 * 2**20
+            collective_id=0, has_side_effects=True, vmem_limit_bytes=60 * 2**20
         ),
     )(density, columns, owner_map)
 

time: 54.8 us -> 51.3 us (0.936); the launches traced: 53.8 us -> 51.1 us
  Pallas kernels: 50.8 us -> 49.4 us
  local copies, waits for them, and re-layouts: 2.99 us -> 1.67 us
    pallas_call x1, Pallas kernels: 50.8 us -> 49.4 us  [gathered(): pl.pallas_call(gather_kernel, out_shape=jax.ShapeDtypeStruct(density.shap...]
    unnamed x7 -> x1, local copies, waits for them, and re-layouts: 2.99 us -> 1.67 us
where the time goes in v2:
time: 51.3 us; the launch traced here: 51.1 us
  Pallas kernels  49.4 us (96%)
  local copies, waits for them, and re-layouts  1.67 us (3%)
    pallas_call x1, Pallas kernels, gathered(): pl.pallas_call(gather_kernel, out_shape=jax.ShapeDtypeStruct(density.shap...  49.4 us
    unnamed x1, local copies, waits for them, and re-layouts  1.67 us

profile of v2, /device:TPU:0, one launch (start us, length us, event | category | flops | bytes accessed | tf_op | source)
XLA Modules:
  0.0 51.1 jit_solution(6004714649610495929)
XLA Ops:
  0.0 49.4 %shard_map.37 = f32[2,1,2,128,128]{4,3,2,1,0:T(8,128)} custom-call(f32[2,1,2,128,128]{4,3,2,1,0:T(8,128)} %den_ref.1, s32[2,1,2]{2,1,0:T(1,128)} %cols_ref.1, s32[16]{0:T(128)} %owner_ref.1), custom_call_target="tpu_custom_call" | custom-call | tf_op jit(solution)/shard_map/pallas_call | solution.py:405
  49.4 1.7 %copy.5 = f32[2,1,2,128,128]{4,3,2,1,0:T(8,128)} copy(f32[2,1,2,128,128]{4,3,2,1,0:T(8,128)} %shard_map.37) | data formatting | bytes 524288
